TPU v7x, 256 devices: a whole 4x4x8 slice. The times are simulated.
256 devices in a mesh: row: 16 (over z_lo, y, core), col: 16 (over z_hi, x).
Axes of the slice: x: 4, y: 4, z: 8 (z_hi: 4, z_lo: 2; z = z_hi * 2 + z_lo), core: 2. Of those that a mesh axis runs over, the one named last changes fastest.
Arguments:
- states_now: float32 [40, 32768], P(None, ('col', 'row')), may hold values from -60 to 60
- states_next: float32 [40, 32768], P(None, ('row', 'col')), may hold values from -60 to 60
- states_last: float32 [40, 32768], P(None, ('col', 'row')), may hold values from -60 to 60
- payoff_now: bfloat16 [64, 32768], P(None, ('col', 'row')), may hold values from 0 to 2
- payoff_next: bfloat16 [64, 32768], P(None, ('row', 'col')), may hold values from 0 to 2
- payoff_last: bfloat16 [64, 32768], P(None, ('col', 'row')), may hold values from 0 to 2
Outputs:
- value_next: float32 [64, 32768], P(None, ('row', 'col'))
- value_now: float32 [64, 32768], P(None, ('col', 'row'))
All inputs are finite; a program needn't handle non-finite values.
Results may differ from a plain program's by a relative error of at most 0.0003.
Values sent between devices are 32-bit elements; how exact they have to be, the bound alone decides.
A program may use at most 128 MiB of HBM per device.

v0:
```python
import math
import jax
import jax.numpy as jnp
from jax import lax
from jax.sharding import PartitionSpec as P


def log_kernel(row_states, col_states, row_norms, col_norms):
    cross_term = lax.dot_general(
        row_states,
        col_states,
        (((0,), (0,)), ((), ())),
        precision=lax.Precision.HIGHEST,
        preferred_element_type=jnp.float32,
    )
    return cross_term - 0.5 * row_norms[:, None] - 0.5 * col_norms[None, :]


def log_blocks(row_states, col_states):
    factors, points = row_states.shape
    block_rows = math.gcd(points, 512)
    block_count = points // block_rows
    blocks = row_states.reshape(factors, block_count, block_rows).transpose(1, 0, 2)
    norms = jnp.sum(row_states * row_states, axis=0).reshape(block_count, block_rows)
    col_norms = jnp.sum(col_states * col_states, axis=0)

    def build(block_item):
        row_piece, piece_norms = block_item
        return log_kernel(row_piece, col_states, piece_norms, col_norms)

    return lax.map(build, (blocks, norms))


def local_stats(log_weight):
    col_peak = jnp.max(log_weight, axis=(0, 1))
    col_sum = jnp.sum(jnp.exp(log_weight - col_peak[None, None, :]), axis=(0, 1))
    return (col_peak, col_sum)


def stats_row(col_peak, col_sum):
    global_peak = lax.pmax(col_peak, "row")
    global_sum = lax.psum(col_sum * jnp.exp(col_peak - global_peak), "row")
    return (global_peak, global_sum)


def continuation(log_weight, later_value, col_peak, col_sum):
    scaled = (later_value / col_sum[None, :]).astype(jnp.bfloat16)

    def project(weight_block):
        kernel = jnp.exp(weight_block - col_peak[None, :]).astype(jnp.bfloat16)
        return lax.dot_general(
            scaled, kernel, (((1,), (1,)), ((), ())), preferred_element_type=jnp.float32
        )

    pieces = lax.map(project, log_weight)
    block_count, block_rows = (log_weight.shape[0], log_weight.shape[1])
    return pieces.transpose(1, 0, 2).reshape(scaled.shape[0], block_count * block_rows)


def per_device(states_now, states_next, states_last, payoff_now, payoff_next, payoff_last):
    later_states, later_values = (
        lax.all_gather(states_last, "row", axis=1, tiled=True),
        lax.all_gather(payoff_last.astype(jnp.float32), "row", axis=1, tiled=True),
    )
    next_rows = lax.all_gather(states_next, "col", axis=1, tiled=True)
    weights = log_blocks(next_rows, later_states)
    col_peak, col_sum = local_stats(weights)
    col_peak, col_sum = stats_row(col_peak, col_sum)
    partial_value = continuation(weights, later_values, col_peak, col_sum)
    own_next = lax.psum_scatter(partial_value, "col", scatter_dimension=1, tiled=True)
    value_next = jnp.maximum(payoff_next.astype(jnp.float32), own_next)
    now_rows = lax.all_gather(states_now, "col", axis=1, tiled=True)
    next_cols, value_cols = (
        lax.all_gather(states_next, "row", axis=1, tiled=True),
        lax.all_gather(value_next, "row", axis=1, tiled=True),
    )
    weights = log_blocks(now_rows, next_cols)
    col_peak, col_sum = local_stats(weights)
    col_peak, col_sum = stats_row(col_peak, col_sum)
    partial_value = continuation(weights, value_cols, col_peak, col_sum)
    own_block = lax.psum_scatter(partial_value, "col", scatter_dimension=1, tiled=True)
    value_now = jnp.maximum(payoff_now.astype(jnp.float32), own_block)
    return (value_next, value_now)


def solution(mesh):
    in_specs = (
        P(None, ("col", "row")),
        P(None, ("row", "col")),
        P(None, ("col", "row")),
        P(None, ("col", "row")),
        P(None, ("row", "col")),
        P(None, ("col", "row")),
    )
    out_specs = (P(None, ("row", "col")), P(None, ("col", "row")))
    return jax.shard_map(
        per_device, mesh=mesh, in_specs=in_specs, out_specs=out_specs, check_vma=False
    )
```

profile of v0, /device:TPU:8, one launch (start us, length us, event | category | flops | bytes accessed | tf_op | source)
XLA Modules:
  0.0 563.3 jit_solution(17174039601657234633)
XLA Ops:
  7.2 0.0 reduce-scatter.3.cloned.1.call-start
  7.2 48.8 %all_gather.21 = f32[40,2048]{1,0:T(8,128)S(1)} all-gather(f32[40,128]{1,0:T(8,128)} %param.14), channel_id=1, replica_groups=mesh['row'=16,'col'=16] {'col'}, dimensions={1}, use_global_device_ids=true | all-gather | bytes 348160 | tf_op jit(solution)/shard_map/all_gather | solution.py:72
  56.0 0.2 reshape.59
  56.2 17.5 %all_gather.22 = f32[40,2048]{1,0:T(8,128)S(1)} all-gather(f32[40,128]{1,0:T(8,128)} %param.15), channel_id=1, replica_groups=mesh['row'=16,'col'=16] {'row'}, dimensions={1}, use_global_device_ids=true | all-gather | bytes 348160 | tf_op jit(solution)/shard_map/all_gather | solution.py:74
  73.7 40.1 %all_gather.18 = f32[40,2048]{1,0:T(8,128)S(1)} all-gather(f32[40,128]{1,0:T(8,128)} %param.15), channel_id=1, replica_groups=mesh['row'=16,'col'=16] {'col'}, dimensions={1}, use_global_device_ids=true | all-gather | bytes 348160 | tf_op jit(solution)/shard_map/all_gather | solution.py:65
  113.8 0.2 reshape.56
  114.1 0.0 copy-start.1
  114.1 7.8 %broadcast.49.clone.1 = f32[4,512,2048]{2,1,0:T(8,128)} broadcast(f32[]{:T(128)} %constant.47.clone.1), dimensions={} | broadcast | bytes 16777220 | tf_op jit(solution)/shard_map/broadcast.11
  122.0 21.0 %while.42 = (s32[]{:T(128)}, f32[4,512,2048]{2,1,0:T(8,128)}, f32[4,40,512]{2,0,1:T(4,128)S(1)}, f32[40,2048]{1,0:T(8,128)S(1)}, f32[4,512]{1,0:T(4,128)S(1)}, /*index=5*/f32[2048]{0:T(1024)S(1)}, s32[]{:T(128)}) while((s32[]{:T(128)}, f32[4,512,2048]{2,1,0:T(8,128)}, f32[4,40,512]{2,0,1:T(4,128)S(1)}, f32[40,2048]{1,0:T(8,128)S(1)}, ...), condition=%wide.region_14.15_spmd, body=%wide.region_13.14_spmd.sunk | while | flops 505416192 | bytes 4799061 | solution.py:31
  122.0 0.1 constant_dynamic-slice_fusion.5
  122.1 5.2 bitcast_dynamic-update-slice_fusion.5
  127.3 0.1 constant_dynamic-slice_fusion.5
  127.4 5.1 bitcast_dynamic-update-slice_fusion.5
  132.5 0.1 constant_dynamic-slice_fusion.5
  132.6 5.2 bitcast_dynamic-update-slice_fusion.5
  137.8 0.1 constant_dynamic-slice_fusion.5
  137.9 5.1 bitcast_dynamic-update-slice_fusion.5
  143.0 0.0 copy-done.1
  143.0 20.0 %all_gather.19 = f32[40,2048]{1,0:T(8,128)S(1)} all-gather(f32[40,128]{1,0:T(8,128)S(1)} %copy-done.1), channel_id=1, replica_groups=mesh['row'=16,'col'=16] {'row'}, dimensions={1}, use_global_device_ids=true | all-gather | bytes 348160 | tf_op jit(solution)/shard_map/all_gather | solution.py:62
  163.0 7.8 %broadcast.49.clone = f32[4,512,2048]{2,1,0:T(8,128)} broadcast(f32[]{:T(128)} %constant.47.clone.1), dimensions={} | broadcast | bytes 16777220 | tf_op jit(solution)/shard_map/broadcast.11
  170.9 21.0 %while.40 = (s32[]{:T(128)}, f32[4,512,2048]{2,1,0:T(8,128)}, f32[4,40,512]{2,0,1:T(4,128)S(1)}, f32[40,2048]{1,0:T(8,128)S(1)}, f32[4,512]{1,0:T(4,128)S(1)}, /*index=5*/f32[2048]{0:T(1024)S(1)}, s32[]{:T(128)}) while((s32[]{:T(128)}, f32[4,512,2048]{2,1,0:T(8,128)}, f32[4,40,512]{2,0,1:T(4,128)S(1)}, f32[40,2048]{1,0:T(8,128)S(1)}, ...), condition=%wide.region_3.4_spmd, body=%wide.region_2.3_spmd.sunk | while | flops 505416192 | bytes 4799061 | solution.py:31
  170.9 0.1 constant_dynamic-slice_fusion.4
  171.0 5.2 bitcast_dynamic-update-slice_fusion.4
  176.1 0.1 constant_dynamic-slice_fusion.4
  176.2 5.1 bitcast_dynamic-update-slice_fusion.4
  181.4 0.1 constant_dynamic-slice_fusion.4
  181.5 5.2 bitcast_dynamic-update-slice_fusion.4
  186.6 0.1 constant_dynamic-slice_fusion.4
  186.8 5.1 bitcast_dynamic-update-slice_fusion.4
  191.9 6.6 %reduce_max.19 = f32[2048]{0:T(1024)S(1)} reduce(f32[4,512,2048]{2,1,0:T(8,128)} %get-tuple-element.384, f32[]{:T(128)} %constant.48.clone.1), dimensions={0,1}, to_apply=%region_15.16 | reduce | flops 4192256 | bytes 16785412 | tf_op jit(solution)/shard_map/reduce_max | solution.py:35
  198.5 6.6 %reduce_max.18 = f32[2048]{0:T(1024)S(1)} reduce(f32[4,512,2048]{2,1,0:T(8,128)} %get-tuple-element.366, f32[]{:T(128)} %constant.48.clone.1), dimensions={0,1}, to_apply=%region_4.5 | reduce | flops 4192256 | bytes 16785412 | tf_op jit(solution)/shard_map/reduce_max | solution.py:35
  205.1 0.0 copy-start.2
  205.1 8.1 %exponential_reduce_fusion = f32[2048]{0:T(1024)S(1)} fusion(f32[4,512,2048]{2,1,0:T(8,128)} %get-tuple-element.384, f32[2048]{0:T(1024)S(1)} %reduce_max.19), kind=kLoop, calls=%fused_computation.24 | loop fusion | flops 8386560 | bytes 16793600 | tf_op jit(solution)/shard_map/reduce_sum | solution.py:36
  213.1 50.4 %all-reduce.1 = (f32[2048]{0:T(1024)S(1)}, f32[2048]{0:T(1024)S(1)}) all-reduce(f32[2048]{0:T(1024)S(1)} %reduce_max.18, f32[2048]{0:T(1024)S(1)} %reduce_max.19), channel_id=1, replica_groups=mesh['row'=16,'col'=16] {'row'}, use_global_device_ids=true, to_apply=%region_5.6 | all-reduce | flops 4096 | bytes 32768 | tf_op jit(solution)/shard_map/pmax | solution.py:41
  263.5 8.1 %exponential_reduce_fusion.1 = f32[2048]{0:T(1024)S(1)} fusion(f32[4,512,2048]{2,1,0:T(8,128)} %get-tuple-element.366, f32[2048]{0:T(1024)S(1)} %reduce_max.18), kind=kLoop, calls=%fused_computation.25 | loop fusion | flops 8386560 | bytes 16793600 | tf_op jit(solution)/shard_map/reduce_sum | solution.py:36
  271.6 0.0 copy-done.2
  271.6 21.7 %all_gather.20 = f32[64,2048]{1,0:T(8,128)S(1)} all-gather(f32[64,128]{1,0:T(8,128)S(1)} %convert_element_type.22), channel_id=1, replica_groups=mesh['row'=16,'col'=16] {'row'}, dimensions={1}, use_global_device_ids=true | all-gather | bytes 557056 | tf_op jit(solution)/shard_map/all_gather | solution.py:63
  293.3 50.4 %all-reduce = (f32[2048]{0:T(1024)S(1)}, f32[2048]{0:T(1024)S(1)}) all-reduce(f32[2048]{0:T(1024)S(1)} %get-tuple-element.185, f32[2048]{0:T(1024)S(1)} %get-tuple-element.184), channel_id=1, replica_groups=mesh['row'=16,'col'=16] {'row'}, use_global_device_ids=true, to_apply=%region_7.8 | all-reduce | flops 4096 | bytes 32768 | tf_op jit(solution)/shard_map/psum | solution.py:42
  343.8 0.1 broadcast.48.clone
  343.8 11.9 %while.41 = (s32[]{:T(128)}, f32[4,64,512]{2,1,0:T(8,128)S(1)}, f32[4,512,2048]{2,1,0:T(8,128)}, f32[2048]{0:T(1024)S(1)}, bf16[64,2048]{1,0:T(8,128)(2,1)S(1)}, /*index=5*/s32[]{:T(128)}) while((s32[]{:T(128)}, f32[4,64,512]{2,1,0:T(8,128)S(1)}, f32[4,512,2048]{2,1,0:T(8,128)}, f32[2048]{0:T(1024)S(1)}, bf16[64,2048]{1,0:T(8,128)(2,1)S(1)}, ...), condition=%wide.region_9.10_spmd, body=%wide.region_8.9_spmd.sunk | while | flops 136314880 | bytes 4596805 | solution.py:55
  343.8 3.0 fusion.37
  346.8 3.0 fusion.37
  349.8 3.0 fusion.37
  352.7 3.0 fusion.37
  355.7 0.0 copy-start.4
  355.7 0.8 copy.16
  356.6 0.0 reduce-scatter.3.cloned.1.call-update
  356.6 0.0 reduce-scatter.5.cloned.1.call-start
  356.6 83.4 %reduce-scatter.3.cloned.1.call-done = f32[64,128]{1,0:T(8,128)} async-done(((f32[64,2048]{1,0:T(8,128)}), f32[64,128]{1,0:T(8,128)}) %reduce-scatter.3.cloned.1.call-update) | async-done | bytes 32784 | tf_op jit(solution)/shard_map/reduce_scatter | solution.py:70
  440.1 0.0 copy-done.3
  440.1 0.8 convert_maximum_fusion.1
  440.9 17.9 %all_gather.23 = f32[64,2048]{1,0:T(8,128)S(1)} all-gather(f32[64,128]{1,0:T(8,128)S(1)} %convert_maximum_fusion.1), channel_id=1, replica_groups=mesh['row'=16,'col'=16] {'row'}, dimensions={1}, use_global_device_ids=true | all-gather | bytes 557056 | tf_op jit(solution)/shard_map/all_gather | solution.py:75
  458.8 0.1 broadcast.48
  458.8 11.9 %while.43 = (s32[]{:T(128)}, f32[4,64,512]{2,1,0:T(8,128)S(1)}, f32[4,512,2048]{2,1,0:T(8,128)}, f32[2048]{0:T(1024)S(1)}, bf16[64,2048]{1,0:T(8,128)(2,1)S(1)}, /*index=5*/s32[]{:T(128)}) while((s32[]{:T(128)}, f32[4,64,512]{2,1,0:T(8,128)S(1)}, f32[4,512,2048]{2,1,0:T(8,128)}, f32[2048]{0:T(1024)S(1)}, bf16[64,2048]{1,0:T(8,128)(2,1)S(1)}, ...), condition=%wide.region_20.21_spmd, body=%wide.region_19.20_spmd.sunk | while | flops 136314880 | bytes 4596805 | solution.py:55
  458.8 3.0 fusion.41
  461.8 3.0 fusion.41
  464.8 3.0 fusion.41
  467.8 3.0 fusion.41
  470.7 0.8 copy.17
  471.6 0.0 reduce-scatter.5.cloned.1.call-update
  471.6 83.5 %reduce-scatter.5.cloned.1.call-done = f32[64,128]{1,0:T(8,128)} async-done(((f32[64,2048]{1,0:T(8,128)}), f32[64,128]{1,0:T(8,128)}) %reduce-scatter.5.cloned.1.call-update) | async-done | bytes 32784 | tf_op jit(solution)/shard_map/reduce_scatter | solution.py:81
  555.1 0.0 copy-done.4
  555.1 1.4 convert_maximum_fusion
  556.4 0.0 copy-done
  (28 shorter events, 0.4 us)
Async XLA Ops:
  7.2 432.9 %reduce-scatter.3.cloned.1.call-start = ((), (), s32[]{:S(2)}) async-start(), calls=%async_computation.2 | async-start | bytes 557056 | tf_op jit(solution)/shard_map/reduce_scatter | solution.py:70
  114.1 28.9 %copy-start.1 = (f32[40,128]{1,0:T(8,128)S(1)}, f32[40,128]{1,0:T(8,128)}, u32[]{:S(2)}) copy-start(f32[40,128]{1,0:T(8,128)} %param.16) | copy-start | bytes 61444
  205.1 66.5 %copy-start.2 = (bf16[64,128]{1,0:T(8,128)(2,1)S(1)}, bf16[64,128]{1,0:T(8,128)(2,1)}, u32[]{:S(2)}) copy-start(bf16[64,128]{1,0:T(8,128)(2,1)} %param.19) | copy-start | bytes 49156
  271.6 168.5 %copy-start.3 = (bf16[64,128]{1,0:T(8,128)(2,1)S(1)}, bf16[64,128]{1,0:T(8,128)(2,1)}, u32[]{:S(2)}) copy-start(bf16[64,128]{1,0:T(8,128)(2,1)} %param.18) | copy-start | bytes 49156
  355.7 199.3 %copy-start.4 = (bf16[64,128]{1,0:T(8,128)(2,1)S(1)}, bf16[64,128]{1,0:T(8,128)(2,1)}, u32[]{:S(2)}) copy-start(bf16[64,128]{1,0:T(8,128)(2,1)} %param.17) | copy-start | bytes 49156
  356.6 198.5 %reduce-scatter.5.cloned.1.call-start = ((), (), s32[]{:S(2)}) async-start(), calls=%async_computation.3 | async-start | bytes 557056 | tf_op jit(solution)/shard_map/reduce_scatter | solution.py:81
  440.9 115.6 %copy-start = (f32[64,128]{1,0:T(8,128)}, f32[64,128]{1,0:T(8,128)S(1)}, u32[]{:S(2)}) copy-start(f32[64,128]{1,0:T(8,128)S(1)} %convert_maximum_fusion.1) | copy-start | bytes 98308
Sparse Core Ops, SparseCore 0:
  356.7 83.3 reduce-scatter.2
  471.7 83.3 reduce-scatter.4
where the time goes:
time: 564 us; the launch traced here: 563 us
  blocking collectives  267 us (47%)
  waiting for transfers between devices  167 us (30%)
  matrix products  64.8 us (11%)
  other arithmetic  31.9 us (6%)
  local copies, waits for them, and re-layouts  18.5 us (3%)
  between operations  14.2 us (3%)
    reduce_scatter x2, waiting for transfers between devices, per_device(): lax.psum_scatter(partial_value, 'col', scatter_dimension=1, tiled=True)  167 us
    psum x1, blocking collectives, stats_row(): global_sum = lax.psum(col_sum * jnp.exp(col_peak - global_peak), 'row')  50.4 us
    pmax x1, blocking collectives, stats_row(): global_peak = lax.pmax(col_peak, 'row')  50.4 us
    all_gather x1, blocking collectives, per_device(): now_rows = lax.all_gather(states_now, 'col', axis=1, tiled=True)  48.8 us
    dot_general x8, matrix products, log_kernel(): lax.dot_general(row_states, col_states, (((0,), (0,)), ((), ())), precisi...  41.2 us
    all_gather x1, blocking collectives, per_device(): next_rows = lax.all_gather(states_next, 'col', axis=1, tiled=True)  40.1 us
    dot_general x8, matrix products, project(): lax.dot_general(scaled, kernel, (((1,), (1,)), ((), ())), preferred_eleme...  23.7 us
    all_gather x1, blocking collectives, per_device(): lax.all_gather(payoff_last.astype(jnp.float32), 'row', axis=1, tiled=True)  21.7 us
  transfers between devices with their start and end apart: 2, of which 2 were waited for; matrix products, arithmetic and copies ran while one was open for 0% of the time, Pallas kernels for 0%

commit v1 on v0

--- a/solution.py
+++ b/solution.py
@@ -39,7 +39,7 @@
 
 def stats_row(col_peak, col_sum):
     global_peak = lax.pmax(col_peak, "row")
-    global_sum = lax.psum(col_sum * jnp.exp(col_peak - global_peak), "row")
+    global_sum = jnp.sum(lax.all_gather(col_sum * jnp.exp(col_peak - global_peak), "row"), axis=0)
     return (global_peak, global_sum)
 
 

time: 564 us -> 528 us (0.936)
  waiting for transfers between devices: 167 us -> 146 us
  blocking collectives: 267 us -> 251 us
    psum x1 -> x0, blocking collectives: 50.4 us -> none  [stats_row(): global_sum = lax.psum(col_sum * jnp.exp(col_peak - global_peak), 'row')]
    all_gather x0 -> x2, blocking collectives: none -> 38.9 us  [stats_row(): lax.all_gather(col_sum * jnp.exp(col_peak - global_peak), 'row')]
    reduce_scatter x2, waiting for transfers between devices: 167 us -> 146 us  [per_device(): lax.psum_scatter(partial_value, 'col', scatter_dimension=1, tiled=True)]
where the time goes in v1:
time: 528 us; the launch traced here: 527 us
  blocking collectives  251 us (48%)
  waiting for transfers between devices  146 us (28%)
  matrix products  64.8 us (12%)
  other arithmetic  31.9 us (6%)
  local copies, waits for them, and re-layouts  18.6 us (4%)
  between operations  14.2 us (3%)
    reduce_scatter x2, waiting for transfers between devices, per_device(): lax.psum_scatter(partial_value, 'col', scatter_dimension=1, tiled=True)  146 us
    pmax x1, blocking collectives, stats_row(): global_peak = lax.pmax(col_peak, 'row')  50.4 us
    all_gather x1, blocking collectives, per_device(): now_rows = lax.all_gather(states_now, 'col', axis=1, tiled=True)  48.8 us
    dot_general x8, matrix products, log_kernel(): lax.dot_general(row_states, col_states, (((0,), (0,)), ((), ())), precisi...  41.2 us
    all_gather x1, blocking collectives, per_device(): next_rows = lax.all_gather(states_next, 'col', axis=1, tiled=True)  40.1 us
    all_gather x2, blocking collectives, stats_row(): lax.all_gather(col_sum * jnp.exp(col_peak - global_peak), 'row')  38.9 us
    dot_general x8, matrix products, project(): lax.dot_general(scaled, kernel, (((1,), (1,)), ((), ())), preferred_eleme...  23.7 us
    all_gather x1, blocking collectives, per_device(): lax.all_gather(states_last, 'row', axis=1, tiled=True)  20 us
  transfers between devices with their start and end apart: 2, of which 2 were waited for; matrix products, arithmetic and copies ran while one was open for 0% of the time, Pallas kernels for 0%

profile of v1, /device:TPU:8, one launch (start us, length us, event | category | flops | bytes accessed | tf_op | source)
XLA Modules:
  0.0 527.0 jit_solution(17912601127806779696)
XLA Ops:
  7.2 0.0 reduce-scatter.3.cloned.1.call-start
  7.2 48.8 %all_gather.35 = f32[40,2048]{1,0:T(8,128)S(1)} all-gather(f32[40,128]{1,0:T(8,128)} %param.14), channel_id=1, replica_groups=mesh['row'=16,'col'=16] {'col'}, dimensions={1}, use_global_device_ids=true | all-gather | bytes 348160 | tf_op jit(solution)/shard_map/all_gather | solution.py:72
  56.0 0.2 reshape.59
  56.2 17.5 %all_gather.36 = f32[40,2048]{1,0:T(8,128)S(1)} all-gather(f32[40,128]{1,0:T(8,128)} %param.15), channel_id=1, replica_groups=mesh['row'=16,'col'=16] {'row'}, dimensions={1}, use_global_device_ids=true | all-gather | bytes 348160 | tf_op jit(solution)/shard_map/all_gather | solution.py:74
  73.7 40.1 %all_gather.30 = f32[40,2048]{1,0:T(8,128)S(1)} all-gather(f32[40,128]{1,0:T(8,128)} %param.15), channel_id=1, replica_groups=mesh['row'=16,'col'=16] {'col'}, dimensions={1}, use_global_device_ids=true | all-gather | bytes 348160 | tf_op jit(solution)/shard_map/all_gather | solution.py:65
  113.8 0.2 reshape.56
  114.1 0.0 copy-start.1
  114.1 7.8 %broadcast.49.clone.1 = f32[4,512,2048]{2,1,0:T(8,128)} broadcast(f32[]{:T(128)} %constant.47.clone.1), dimensions={} | broadcast | bytes 16777220 | tf_op jit(solution)/shard_map/broadcast.11
  122.0 21.0 %while.42 = (s32[]{:T(128)}, f32[4,512,2048]{2,1,0:T(8,128)}, f32[4,40,512]{2,0,1:T(4,128)S(1)}, f32[40,2048]{1,0:T(8,128)S(1)}, f32[4,512]{1,0:T(4,128)S(1)}, /*index=5*/f32[2048]{0:T(1024)S(1)}, s32[]{:T(128)}) while((s32[]{:T(128)}, f32[4,512,2048]{2,1,0:T(8,128)}, f32[4,40,512]{2,0,1:T(4,128)S(1)}, f32[40,2048]{1,0:T(8,128)S(1)}, ...), condition=%wide.region_14.15_spmd, body=%wide.region_13.14_spmd.sunk | while | flops 505416192 | bytes 4799061 | solution.py:31
  122.0 0.1 constant_dynamic-slice_fusion.5
  122.1 5.2 bitcast_dynamic-update-slice_fusion.5
  127.3 0.1 constant_dynamic-slice_fusion.5
  127.4 5.1 bitcast_dynamic-update-slice_fusion.5
  132.5 0.1 constant_dynamic-slice_fusion.5
  132.6 5.2 bitcast_dynamic-update-slice_fusion.5
  137.8 0.1 constant_dynamic-slice_fusion.5
  137.9 5.1 bitcast_dynamic-update-slice_fusion.5
  143.0 0.0 copy-done.1
  143.0 20.0 %all_gather.31 = f32[40,2048]{1,0:T(8,128)S(1)} all-gather(f32[40,128]{1,0:T(8,128)S(1)} %copy-done.1), channel_id=1, replica_groups=mesh['row'=16,'col'=16] {'row'}, dimensions={1}, use_global_device_ids=true | all-gather | bytes 348160 | tf_op jit(solution)/shard_map/all_gather | solution.py:62
  163.0 7.8 %broadcast.49.clone = f32[4,512,2048]{2,1,0:T(8,128)} broadcast(f32[]{:T(128)} %constant.47.clone.1), dimensions={} | broadcast | bytes 16777220 | tf_op jit(solution)/shard_map/broadcast.11
  170.9 21.0 %while.40 = (s32[]{:T(128)}, f32[4,512,2048]{2,1,0:T(8,128)}, f32[4,40,512]{2,0,1:T(4,128)S(1)}, f32[40,2048]{1,0:T(8,128)S(1)}, f32[4,512]{1,0:T(4,128)S(1)}, /*index=5*/f32[2048]{0:T(1024)S(1)}, s32[]{:T(128)}) while((s32[]{:T(128)}, f32[4,512,2048]{2,1,0:T(8,128)}, f32[4,40,512]{2,0,1:T(4,128)S(1)}, f32[40,2048]{1,0:T(8,128)S(1)}, ...), condition=%wide.region_3.4_spmd, body=%wide.region_2.3_spmd.sunk | while | flops 505416192 | bytes 4799061 | solution.py:31
  170.9 0.1 constant_dynamic-slice_fusion.4
  171.0 5.2 bitcast_dynamic-update-slice_fusion.4
  176.1 0.1 constant_dynamic-slice_fusion.4
  176.2 5.1 bitcast_dynamic-update-slice_fusion.4
  181.4 0.1 constant_dynamic-slice_fusion.4
  181.5 5.2 bitcast_dynamic-update-slice_fusion.4
  186.6 0.1 constant_dynamic-slice_fusion.4
  186.8 5.1 bitcast_dynamic-update-slice_fusion.4
  191.9 6.6 %reduce_max.19 = f32[2048]{0:T(1024)S(1)} reduce(f32[4,512,2048]{2,1,0:T(8,128)} %get-tuple-element.406, f32[]{:T(128)} %constant.48.clone.1), dimensions={0,1}, to_apply=%region_15.16 | reduce | flops 4192256 | bytes 16785412 | tf_op jit(solution)/shard_map/reduce_max | solution.py:35
  198.5 6.6 %reduce_max.18 = f32[2048]{0:T(1024)S(1)} reduce(f32[4,512,2048]{2,1,0:T(8,128)} %get-tuple-element.388, f32[]{:T(128)} %constant.48.clone.1), dimensions={0,1}, to_apply=%region_4.5 | reduce | flops 4192256 | bytes 16785412 | tf_op jit(solution)/shard_map/reduce_max | solution.py:35
  205.1 8.1 %exponential_reduce_fusion = f32[2048]{0:T(1024)S(1)} fusion(f32[4,512,2048]{2,1,0:T(8,128)} %get-tuple-element.406, f32[2048]{0:T(1024)S(1)} %reduce_max.19), kind=kLoop, calls=%fused_computation.24 | loop fusion | flops 8386560 | bytes 16793600 | tf_op jit(solution)/shard_map/reduce_sum | solution.py:36
  213.1 50.4 %all-reduce = (f32[2048]{0:T(1024)S(1)}, f32[2048]{0:T(1024)S(1)}) all-reduce(f32[2048]{0:T(1024)S(1)} %reduce_max.18, f32[2048]{0:T(1024)S(1)} %reduce_max.19), channel_id=1, replica_groups=mesh['row'=16,'col'=16] {'row'}, use_global_device_ids=true, to_apply=%region_5.6 | all-reduce | flops 4096 | bytes 32768 | tf_op jit(solution)/shard_map/pmax | solution.py:41
  263.5 8.1 %exponential_reduce_fusion.1 = f32[2048]{0:T(1024)S(1)} fusion(f32[4,512,2048]{2,1,0:T(8,128)} %get-tuple-element.388, f32[2048]{0:T(1024)S(1)} %reduce_max.18), kind=kLoop, calls=%fused_computation.25 | loop fusion | flops 8386560 | bytes 16793600 | tf_op jit(solution)/shard_map/reduce_sum | solution.py:36
  271.6 20.6 %all-gather = f32[32768]{0:T(1024)S(1)} all-gather(f32[2048]{0:T(1024)S(1)} %get-tuple-element.207), channel_id=2, replica_groups=mesh['row'=16,'col'=16] {'row'}, dimensions={0}, use_global_device_ids=true | all-gather | bytes 139264 | tf_op jit(solution)/shard_map/all_gather | solution.py:42
  292.3 0.0 copy-done.2
  292.3 17.4 %all_gather.32 = f32[64,2048]{1,0:T(8,128)S(1)} all-gather(f32[64,128]{1,0:T(8,128)S(1)} %convert_element_type.22), channel_id=1, replica_groups=mesh['row'=16,'col'=16] {'row'}, dimensions={1}, use_global_device_ids=true | all-gather | bytes 557056 | tf_op jit(solution)/shard_map/all_gather | solution.py:63
  309.8 0.1 broadcast.48.clone
  309.8 11.9 %while.41 = (s32[]{:T(128)}, f32[4,64,512]{2,1,0:T(8,128)S(1)}, f32[4,512,2048]{2,1,0:T(8,128)}, f32[2048]{0:T(1024)S(1)}, bf16[64,2048]{1,0:T(8,128)(2,1)S(1)}, /*index=5*/s32[]{:T(128)}) while((s32[]{:T(128)}, f32[4,64,512]{2,1,0:T(8,128)S(1)}, f32[4,512,2048]{2,1,0:T(8,128)}, f32[2048]{0:T(1024)S(1)}, bf16[64,2048]{1,0:T(8,128)(2,1)S(1)}, ...), condition=%wide.region_9.10_spmd, body=%wide.region_8.9_spmd.sunk | while | flops 136314880 | bytes 4596805 | solution.py:55
  309.8 3.0 fusion.37
  312.8 3.0 fusion.37
  315.8 3.0 fusion.37
  318.8 3.0 fusion.37
  321.7 0.0 copy-start.4
  321.7 0.8 copy.24
  322.6 0.0 reduce-scatter.3.cloned.1.call-update
  322.6 0.0 reduce-scatter.5.cloned.1.call-start
  322.7 18.3 %all-gather.1 = f32[32768]{0:T(1024)S(1)} all-gather(f32[2048]{0:T(1024)S(1)} %get-tuple-element.206), channel_id=3, replica_groups=mesh['row'=16,'col'=16] {'row'}, dimensions={0}, use_global_device_ids=true | all-gather | bytes 139264 | tf_op jit(solution)/shard_map/all_gather | solution.py:42
  341.0 62.7 %reduce-scatter.3.cloned.1.call-done = f32[64,128]{1,0:T(8,128)} async-done(((f32[64,2048]{1,0:T(8,128)}), f32[64,128]{1,0:T(8,128)}) %reduce-scatter.3.cloned.1.call-update) | async-done | bytes 32784 | tf_op jit(solution)/shard_map/reduce_scatter | solution.py:70
  403.7 0.0 copy-done.3
  403.7 0.8 convert_maximum_fusion.1
  404.5 17.9 %all_gather.37 = f32[64,2048]{1,0:T(8,128)S(1)} all-gather(f32[64,128]{1,0:T(8,128)S(1)} %convert_maximum_fusion.1), channel_id=1, replica_groups=mesh['row'=16,'col'=16] {'row'}, dimensions={1}, use_global_device_ids=true | all-gather | bytes 557056 | tf_op jit(solution)/shard_map/all_gather | solution.py:75
  422.4 0.1 broadcast.48
  422.5 11.9 %while.43 = (s32[]{:T(128)}, f32[4,64,512]{2,1,0:T(8,128)S(1)}, f32[4,512,2048]{2,1,0:T(8,128)}, f32[2048]{0:T(1024)S(1)}, bf16[64,2048]{1,0:T(8,128)(2,1)S(1)}, /*index=5*/s32[]{:T(128)}) while((s32[]{:T(128)}, f32[4,64,512]{2,1,0:T(8,128)S(1)}, f32[4,512,2048]{2,1,0:T(8,128)}, f32[2048]{0:T(1024)S(1)}, bf16[64,2048]{1,0:T(8,128)(2,1)S(1)}, ...), condition=%wide.region_20.21_spmd, body=%wide.region_19.20_spmd.sunk | while | flops 136314880 | bytes 4596805 | solution.py:55
  422.5 3.0 fusion.41
  425.5 3.0 fusion.41
  428.4 3.0 fusion.41
  431.4 3.0 fusion.41
  434.4 0.8 copy.25
  435.2 0.0 reduce-scatter.5.cloned.1.call-update
  435.3 83.6 %reduce-scatter.5.cloned.1.call-done = f32[64,128]{1,0:T(8,128)} async-done(((f32[64,2048]{1,0:T(8,128)}), f32[64,128]{1,0:T(8,128)}) %reduce-scatter.5.cloned.1.call-update) | async-done | bytes 32784 | tf_op jit(solution)/shard_map/reduce_scatter | solution.py:81
  518.8 0.0 copy-done.4
  518.8 1.4 convert_maximum_fusion
  520.2 0.0 copy-done
  (33 shorter events, 0.5 us)
Async XLA Ops:
  7.2 396.6 %reduce-scatter.3.cloned.1.call-start = ((), (), s32[]{:S(2)}) async-start(), calls=%async_computation.2 | async-start | bytes 557056 | tf_op jit(solution)/shard_map/reduce_scatter | solution.py:70
  114.1 28.9 %copy-start.1 = (f32[40,128]{1,0:T(8,128)S(1)}, f32[40,128]{1,0:T(8,128)}, u32[]{:S(2)}) copy-start(f32[40,128]{1,0:T(8,128)} %param.16) | copy-start | bytes 61444
  205.1 87.2 %copy-start.2 = (bf16[64,128]{1,0:T(8,128)(2,1)S(1)}, bf16[64,128]{1,0:T(8,128)(2,1)}, u32[]{:S(2)}) copy-start(bf16[64,128]{1,0:T(8,128)(2,1)} %param.19) | copy-start | bytes 49156
  271.6 132.1 %copy-start.3 = (bf16[64,128]{1,0:T(8,128)(2,1)S(1)}, bf16[64,128]{1,0:T(8,128)(2,1)}, u32[]{:S(2)}) copy-start(bf16[64,128]{1,0:T(8,128)(2,1)} %param.18) | copy-start | bytes 49156
  321.7 197.1 %copy-start.4 = (bf16[64,128]{1,0:T(8,128)(2,1)S(1)}, bf16[64,128]{1,0:T(8,128)(2,1)}, u32[]{:S(2)}) copy-start(bf16[64,128]{1,0:T(8,128)(2,1)} %param.17) | copy-start | bytes 49156
  322.6 196.2 %reduce-scatter.5.cloned.1.call-start = ((), (), s32[]{:S(2)}) async-start(), calls=%async_computation.3 | async-start | bytes 557056 | tf_op jit(solution)/shard_map/reduce_scatter | solution.py:81
  404.5 115.7 %copy-start = (f32[64,128]{1,0:T(8,128)}, f32[64,128]{1,0:T(8,128)S(1)}, u32[]{:S(2)}) copy-start(f32[64,128]{1,0:T(8,128)S(1)} %convert_maximum_fusion.1) | copy-start | bytes 98308
Sparse Core Ops, SparseCore 0:
  322.7 80.9 reduce-scatter.2
  435.4 83.3 reduce-scatter.4
